TPU v7x, 128 devices: a whole 4x4x4 slice. The times are simulated.
128 devices in a mesh: row: 16 (over z, x), col: 8 (over y, core).
Axes of the slice: x: 4, y: 4, z: 4, core: 2. Of those that a mesh axis runs over, the one named last changes fastest.
Arguments:
- features: float32 [32, 49152], P(None, ('row', 'col')), may hold values from -6 to 6
- lengthscale: float32 [32], replicated, may hold values from 1.5 to 6
- targets: float32 [64, 49152], P(None, ('row', 'col')), may hold values from -15 to 15, as said below
- mask: int32 [64, 49152], P(None, ('row', 'col')), may hold values from 0 to 1, as said below
Outputs:
- solution: float32 [64, 49152], P(None, ('row', 'col'))
- residual: float32 [64, 49152], P(None, ('row', 'col'))
Inputs may be any that keep to these rules, and one draw needn't show every extreme that they name: `targets`: values scaled per configuration. `mask`: for each configuration the observed epochs are a prefix of 1 to 64 epochs; some configuration has all 64.
All inputs are finite; a program needn't handle non-finite values.
Results may differ from a plain program's by a relative error of at most 0.013.
Values may be sent and summed in bfloat16 or wider, within the bound.
No kernel may reach another device: no remote copies, remote signals or barrier semaphores. Data moves between devices by JAX's collectives and lax.ppermute only.
A program may use at most 64 MiB of HBM per device.

v0:
```python
import functools
import math

import jax
import jax.numpy as jnp
from jax import lax
from jax.experimental import pallas as pl
from jax.experimental.pallas import tpu as pltpu
from jax.sharding import PartitionSpec as P

noise_level = 0.5
AGAIN = 2
FAT = 8
COL = ("y", "core")
VMEM = pl.BlockSpec(memory_space=pltpu.VMEM)
bf16 = jnp.bfloat16
f32 = jnp.float32


def params(mib, **more):
    return pltpu.CompilerParams(vmem_limit_bytes=mib << 20, **more)


def epoch_kernel(epochs, total_count):
    s = lax.broadcasted_iota(jnp.int32, (epochs, epochs), 0)
    t = lax.broadcasted_iota(jnp.int32, (epochs, epochs), 1)
    gap = jnp.abs(s - t).astype(f32)
    return (8.0 / math.sqrt(total_count)) * jnp.exp(-gap / (epochs / 4.0))


def epoch_product(field, total_count):
    kernel_t = epoch_kernel(field.shape[0], total_count)
    return jnp.dot(
        kernel_t, field, precision=lax.Precision.HIGHEST, preferred_element_type=f32
    )


def prepare_kernel(
    total_count, feat_in, scale_in, target_in, mask_in, feats_ref, out_ref,
    feat_ref, scale_ref, target_ref, mask_ref, pack, sem, feats_sem, load_sem,
):
    loads = [
        pltpu.make_async_copy(source, target, load_sem.at[place])
        for place, (source, target) in enumerate(
            (
                (scale_in, scale_ref),
                (feat_in, feat_ref),
                (target_in, target_ref),
                (mask_in, mask_ref),
            )
        )
    ]
    for load in loads:
        load.start()
    count = feat_ref.shape[0]
    loads[0].wait()
    across = lax.broadcasted_iota(jnp.int32, (count, count), 0)
    down = lax.broadcasted_iota(jnp.int32, (count, count), 1)
    scale = jnp.sum(jnp.where(across == down, scale_ref[...], 0.0), axis=1, keepdims=True)
    loads[1].wait()
    scaled = feat_ref[...] / scale * math.sqrt(math.log2(math.e))
    high = scaled.astype(bf16)
    low = (scaled - high.astype(f32)).astype(bf16)
    pack[0:count, :] = high
    pack[count : 2 * count, :] = low
    feats_copy = pltpu.make_async_copy(pack.at[0 : 2 * count], feats_ref, feats_sem)
    feats_copy.start()
    loads[2].wait()
    loads[3].wait()
    start = target_ref[...] * mask_ref[...].astype(f32)
    pack[2 * count :, :] = epoch_product(start, total_count).astype(bf16)
    send_all(pack, out_ref, sem)
    feats_copy.wait()


def send_all(source, out_ref, sem):
    copies = [
        pltpu.make_async_copy(source, out_ref.at[place], sem.at[place])
        for place in range(out_ref.shape[0])
    ]
    for copy in copies:
        copy.start()
    for copy in copies:
        copy.wait()


def norm_parts(feats):
    count = feats.shape[0] // 2
    whole = feats[:count, :].astype(f32) + feats[count:, :].astype(f32)
    norm = -0.5 * jnp.sum(whole * whole, axis=0, keepdims=True)
    first = norm.astype(bf16).astype(f32)
    second = (norm - first).astype(bf16).astype(f32)
    third = norm - first - second
    return first, second, third


def block_kernel(
    step_rows, row_ref, col_ref, tile_ref, right, tail_ref, mine_ref, other_ref,
    left, fields, part_ref,
):
    step = pl.program_id(0)
    blocks, epochs, width = part_ref.shape
    count = row_ref.shape[1] // 2
    total = part_ref

    def rows(*parts):
        blank = jnp.zeros((16 - len(parts), width), f32)
        return jnp.concatenate(list(parts) + [blank], axis=0).astype(bf16)

    @pl.when(step == 0)
    def _():
        one = jnp.ones((1, width), f32)
        for block in range(row_ref.shape[0]):
            at = slice(block * width, (block + 1) * width)
            feats = row_ref[block]
            first, second, third = norm_parts(feats)
            right[0 : 2 * count, at] = feats
            right[2 * count : 4 * count, at] = feats
            right[4 * count :, at] = rows(one, one, one, first, second, third)
        for block in range(col_ref.shape[0]):
            at = slice(block * width, (block + 1) * width)
            feats = col_ref[block, 0 : 2 * count, :]
            first, second, third = norm_parts(feats)
            high = feats[0:count, :]
            low = feats[count:, :]
            left[0:count, at] = high
            left[count : 2 * count, at] = high
            left[2 * count : 3 * count, at] = low
            left[3 * count : 4 * count, at] = low
            left[4 * count :, at] = rows(first, second, third, one, one, one)
            fields[:, at] = col_ref[block, 2 * count :, :]
        part_ref[...] = jnp.zeros_like(part_ref)
        tail_ref[...] = left[:, left.shape[1] - tail_ref.shape[1] :]

    at = pl.ds(pl.multiple_of(step * step_rows, step_rows), step_rows)
    power = lax.dot_general(
        left[:, at], right[...], (((0,), (0,)), ((), ())), preferred_element_type=f32
    )
    tile = jnp.exp2(power).astype(bf16)
    tile_ref[...] = tile
    spread = jnp.dot(fields[:, at], tile, preferred_element_type=f32)
    for block in range(blocks):
        part_ref[block] += spread[:, block * width : (block + 1) * width]

    @pl.when(step == pl.num_programs(0) - 1)
    def _():
        split_parts(part_ref, mine_ref, other_ref)


def split_parts(part_ref, mine_ref, other_ref):
    core = lax.axis_index("core")
    epochs = part_ref.shape[1]
    for place in range(mine_ref.shape[0]):
        mine_ref[place, 0:epochs, :] = part_ref[2 * place + core]
        other_ref[place, 0:epochs, :] = part_ref[2 * place + 1 - core]


def add_kernel(mine_ref, other_ref, *out_refs):
    count = mine_ref.shape[0]
    epochs = out_refs[0].shape[0]
    here = lax.axis_index("y")
    for shift, out_ref in enumerate(out_refs[:count]):
        place = lax.rem(here + shift, count)
        out_ref[...] = mine_ref[place, 0:epochs, :] + other_ref[place, 0:epochs, :]
    for sums_ref in out_refs[count:]:
        row = mine_ref[0, epochs:, 0:128] + other_ref[0, epochs:, 0:128]
        sums_ref[...] = jnp.broadcast_to(row[None], sums_ref.shape)


def pair_sum(mine, other, block, *more):
    count = mine.shape[0]
    other = lax.ppermute(other, "core", [(0, 1), (1, 0)])
    return pl.pallas_call(
        add_kernel,
        out_shape=(block,) * count + more,
        in_specs=[VMEM] * 2,
        out_specs=[VMEM] * (count + len(more)),
        compiler_params=params(8),
    )(mine, other)


def exchange(terms):
    count = len(terms)
    return [
        lax.ppermute(term, "y", [(k, (k + shift) % count) for k in range(count)])
        if shift
        else term
        for shift, term in enumerate(terms)
    ]


def middle_kernel(
    total_count, *refs
):
    *part_refs, target_ref, mask_ref, image_ref, out_ref, sums_ref, pack, sem = refs
    observed = mask_ref[...].astype(f32)
    start = target_ref[...] * observed
    image = observed * sum(part_ref[...] for part_ref in part_refs)
    image_ref[...] = image
    pack[...] = epoch_product(image, total_count).astype(bf16)
    send_all(pack, out_ref, sem)
    sums_ref[...] = lanes(
        jnp.sum(start * start), jnp.sum(start * image), jnp.sum(image * image)
    )


def lanes(*values):
    lane = lax.broadcasted_iota(jnp.int32, (1, 128), 1)
    row = jnp.zeros((1, 128), f32)
    for place, value in enumerate(values):
        row = jnp.where(lane == place, value, row)
    return row


def again_kernel(
    step_rows, tile_ref, right_ref, left_ref, col_ref, image_ref, sums_ref, mine_ref, other_ref,
    held, fields, part_ref, sem,
):
    blocks, epochs, width = part_ref.shape
    steps = held.shape[0] // step_rows

    def load(step):
        at = pl.ds(pl.multiple_of(step * step_rows, step_rows), step_rows)
        return pltpu.make_async_copy(tile_ref.at[at], held.at[at], sem.at[step])

    for step in range(steps):
        load(step).start()
    for block in range(col_ref.shape[0]):
        fields[:, block * width : (block + 1) * width] = col_ref[block]
    part_ref[...] = jnp.zeros_like(part_ref)

    def add(at, tile):
        spread = jnp.dot(fields[:, at], tile, preferred_element_type=f32)
        for block in range(blocks):
            part_ref[block] += spread[:, block * width : (block + 1) * width]

    def again(step, carry):
        at = pl.ds(pl.multiple_of(step * step_rows, step_rows), step_rows)
        power = lax.dot_general(
            left_ref[:, at], right_ref[...], (((0,), (0,)), ((), ())), preferred_element_type=f32
        )
        at = pl.ds(pl.multiple_of(held.shape[0] + step * step_rows, step_rows), step_rows)
        add(at, jnp.exp2(power).astype(bf16))
        return carry

    def body(step, carry):
        load(step).wait()
        at = pl.ds(pl.multiple_of(step * step_rows, step_rows), step_rows)
        add(at, held[at, :])
        return carry

    lax.fori_loop(0, left_ref.shape[1] // step_rows, again, 0)

    lax.fori_loop(0, steps, body, 0)
    split_parts(part_ref, mine_ref, other_ref)
    cross = jnp.zeros((epochs, width), f32)
    for block in range(blocks):
        cross = cross + part_ref[block] * image_ref[block]
    row = sums_ref[...] + lanes(0.0, 0.0, 0.0, jnp.sum(cross))
    for half_ref in (mine_ref, other_ref):
        half_ref[0, epochs:, 0:128] = jnp.broadcast_to(row, (8, 128))


def finish_kernel(*refs):
    *part_refs, sums_ref, image_ref, target_ref, mask_ref, sol_ref, res_ref = refs
    observed = mask_ref[...].astype(f32)
    start = target_ref[...] * observed
    image = image_ref[...]
    second = observed * sum(part_ref[...] for part_ref in part_refs)
    totals = jnp.sum(sums_ref[...], axis=0)[0:1]
    b00, b01 = totals[:, 0:1], totals[:, 1:2]
    b11, b12 = totals[:, 2:3], totals[:, 3:4]
    mean = b01 / b00
    alpha = 1.0 / (mean + noise_level)
    residual = alpha * (mean * start - image)
    now = alpha * alpha * (b11 - mean * b01)
    beta = now / b00
    direction = residual + beta * start
    moved = (alpha * mean + beta) * image - alpha * second + noise_level * direction
    quad = alpha * alpha * (b12 - 2.0 * mean * b11 + mean * mean * b01)
    mixed = alpha * (mean * b01 - b11)
    curve = quad + 2.0 * beta * mixed + beta * beta * b01
    curve = curve + noise_level * (now + beta * beta * b00)
    step = now / curve
    sol_ref[...] = alpha * start + step * direction
    res_ref[...] = residual - step * moved


def shards(features, lengthscale, targets, mask):
    rows, ys, cores = (lax.axis_size(name) for name in ("row", "y", "core"))
    cols = ys * cores
    epochs, width = targets.shape
    feat = features.shape[0]
    total_count = width * rows * cols
    field = jax.ShapeDtypeStruct((epochs, width), f32)
    sums_shape = jax.ShapeDtypeStruct((1, 128), f32)
    half_shape = jax.ShapeDtypeStruct((ys, epochs, width), f32)
    half_more = jax.ShapeDtypeStruct((ys, epochs + 8, width), f32)
    part_scratch = pltpu.VMEM((cols, epochs, width), f32)
    away = pl.BlockSpec(memory_space=pl.ANY)
    hbm = pl.BlockSpec(memory_space=pltpu.HBM)
    pack_rows = 2 * feat + epochs

    feats, pack = pl.pallas_call(
        functools.partial(prepare_kernel, total_count),
        out_shape=(
            jax.ShapeDtypeStruct((2 * feat, width), bf16),
            jax.ShapeDtypeStruct((rows, pack_rows, width), bf16),
        ),
        in_specs=[hbm] * 4,
        out_specs=[away, away],
        scratch_shapes=[
            pltpu.VMEM((feat, width), f32),
            pltpu.VMEM((1, feat), f32),
            pltpu.VMEM((epochs, width), f32),
            pltpu.VMEM((epochs, width), jnp.int32),
            pltpu.VMEM((pack_rows, width), bf16),
            pltpu.SemaphoreType.DMA((rows,)),
            pltpu.SemaphoreType.DMA,
            pltpu.SemaphoreType.DMA((4,)),
        ],
        compiler_params=params(60),
    )(features, lengthscale[None, :], targets, mask)

    col_pack = lax.all_to_all(pack, "row", 0, 0)
    row_feats = lax.all_gather(feats, COL)

    step_rows = 768
    depth = 4 * feat + 16
    tail = AGAIN * step_rows
    tile, right, left, mine, other = pl.pallas_call(
        functools.partial(block_kernel, step_rows),
        grid=(rows * width // step_rows,),
        out_shape=(
            jax.ShapeDtypeStruct((rows * width, cols * width), bf16),
            jax.ShapeDtypeStruct((depth, cols * width), bf16),
            jax.ShapeDtypeStruct((depth, tail), bf16),
            half_shape,
            half_shape,
        ),
        in_specs=[VMEM] * 2,
        out_specs=[pl.BlockSpec((step_rows, cols * width), lambda s: (s, 0))] + [VMEM] * 4,
        scratch_shapes=[
            pltpu.VMEM((depth, rows * width), bf16),
            pltpu.VMEM((epochs, rows * width), bf16),
            part_scratch,
        ],
        compiler_params=params(48),
    )(row_feats, col_pack)

    terms = exchange(pair_sum(mine, other, field))
    image, pack, sums = pl.pallas_call(
        functools.partial(middle_kernel, total_count),
        out_shape=(field, jax.ShapeDtypeStruct((rows, epochs, width), bf16), sums_shape),
        in_specs=[VMEM] * (len(terms) + 2),
        out_specs=[VMEM, away, VMEM],
        scratch_shapes=[
            pltpu.VMEM((epochs, width), bf16),
            pltpu.SemaphoreType.DMA((rows,)),
        ],
        compiler_params=params(8),
    )(*terms, targets, mask)
    col_weighted = lax.all_to_all(pack, "row", 0, 0)
    row_images = lax.all_gather(image, COL)

    again_rows = 768
    held_rows = rows * width - tail
    mine, other = pl.pallas_call(
        functools.partial(again_kernel, again_rows),
        out_shape=(half_more,) * 2,
        in_specs=[away] + [VMEM] * 5,
        out_specs=[VMEM] * 2,
        scratch_shapes=[
            pltpu.VMEM((held_rows, cols * width), bf16),
            pltpu.VMEM((epochs, rows * width), bf16),
            part_scratch,
            pltpu.SemaphoreType.DMA((held_rows // again_rows,)),
        ],
        compiler_params=params(50),
    )(tile, right, left, col_weighted, row_images, sums)

    *terms, sums = pair_sum(
        mine, other, field, jax.ShapeDtypeStruct((rows * ys, FAT, 128), f32)
    )
    sums = lax.all_to_all(sums, ("row", "y"), 0, 0)
    terms = exchange(terms)
    return pl.pallas_call(
        finish_kernel,
        out_shape=(field, field),
        in_specs=[VMEM] * (len(terms) + 4),
        out_specs=[VMEM] * 2,
        compiler_params=params(8),
    )(*terms, sums, image, targets, mask)


def solution(mesh):
    rows, cols = mesh.devices.shape
    split = jax.sharding.Mesh(mesh.devices.reshape(rows, cols // 2, 2), ("row",) + COL)
    whole = P(None, ("row",) + COL)
    return jax.shard_map(
        shards,
        mesh=split,
        in_specs=(whole, P(), whole, whole),
        out_specs=(whole, whole),
        check_vma=False,
    )
```

profile of v0, /device:TPU:1, one launch (start us, length us, event | category | flops | bytes accessed | tf_op | source)
XLA Modules:
  0.0 122.0 jit_solution(14488440241230195453)
XLA Ops:
  0.6 2.5 %shard_map.59 = (bf16[64,384]{1,0:T(8,128)(2,1)}, bf16[16,128,384]{2,1,0:T(8,128)(2,1)}) custom-call(f32[32,384]{1,0:T(8,128)} %feat_in.1, f32[1,32]{1,0:T(1,128)} %bitcast.5, f32[64,384]{1,0:T(8,128)} %refs_6_.1, s32[64,384]{1,0:T(8,128)} %refs_7_.1), custom_call_target="tpu_custom_call" | custom-call | tf_op jit(solution)/shard_map/pallas_call | solution.py:304
  3.2 8.6 %all-to-all-start = ((bf16[16,128,384]{2,1,0:T(8,128)(2,1)}), bf16[16,128,384]{2,1,0:T(8,128)(2,1)S(1)}, u32[]{:S(2)}, u32[]{:S(2)}) async-start(bf16[16,128,384]{2,1,0:T(8,128)(2,1)} %get-tuple-element.24), calls=%async_computation | async-start | bytes 3145728 | tf_op jit(solution)/shard_map/all_to_all | solution.py:325
  11.8 14.4 %all-gather = bf16[512,384]{1,0:T(8,128)(2,1)S(1)} all-gather(bf16[64,384]{1,0:T(8,128)(2,1)S(1)} %copy-done.2), channel_id=2, replica_groups=mesh['row'=16,'y'=4,'core'=2] {'y','core'}, dimensions={0}, use_global_device_ids=true | all-gather | bytes 442368 | tf_op jit(solution)/shard_map/all_gather | solution.py:326
  26.2 8.4 %all-to-all-done.col_ref = bf16[16,128,384]{2,1,0:T(8,128)(2,1)S(1)} async-done(((bf16[16,128,384]{2,1,0:T(8,128)(2,1)}), bf16[16,128,384]{2,1,0:T(8,128)(2,1)S(1)}, u32[]{:S(2)}, u32[]{:S(2)}) %all-to-all-start) | async-done | bytes 1572896 | tf_op jit(solution)/shard_map/all_to_all | solution.py:325
  34.7 20.9 %shard_map.60 = (bf16[6144,3072]{1,0:T(8,128)(2,1)}, bf16[144,3072]{1,0:T(8,128)(2,1)S(1)}, bf16[144,1536]{1,0:T(8,128)(2,1)S(1)}, f32[4,64,384]{2,1,0:T(8,128)S(1)}, f32[4,64,384]{2,1,0:T(8,128)S(1)}) custom-call(bf16[8,64,384]{2,1,0:T(8,128)(2,1)S(1)} %bitcast.4, bf16[16,128,384]{2,1,0:T(8,128)(2,1)S(1)} %all-to-all-done.col_ref), custom_call_target="tpu_custom_call" | custom-call | tf_op jit(solution)/shard_map/pallas_call | solution.py:331
  55.5 2.5 %collective-permute-start = (f32[4,64,384]{2,1,0:T(8,128)S(1)}, f32[4,64,384]{2,1,0:T(8,128)S(1)}, u32[]{:S(2)}, u32[]{:S(2)}) collective-permute-start(f32[4,64,384]{2,1,0:T(8,128)S(1)} %get-tuple-element.29), channel_id=1, source_target_pairs={{0,1},{1,0},{2,3},{3,2},{4,5},{5,4},{6,7},{7,6},{8,9},{9,8},{10,11... | collective-permute-start | bytes 1179656 | tf_op jit(solution)/shard_map/ppermute | solution.py:172
  58.1 1.3 %collective-permute-done.other_ref = f32[4,64,384]{2,1,0:T(8,128)S(1)} collective-permute-done((f32[4,64,384]{2,1,0:T(8,128)S(1)}, f32[4,64,384]{2,1,0:T(8,128)S(1)}, u32[]{:S(2)}, u32[]{:S(2)}) %collective-permute-start) | collective-permute-done | bytes 393248 | tf_op jit(solution)/shard_map/ppermute | solution.py:172
  59.4 1.4 %collective-permute-start.1 = (f32[64,384]{1,0:T(8,128)S(1)}, f32[64,384]{1,0:T(8,128)S(1)}, u32[]{:S(2)}, u32[]{:S(2)}) collective-permute-start(f32[64,384]{1,0:T(8,128)S(1)} %get-tuple-element.31), channel_id=1, source_target_pairs={{0,2},{2,4},{4,6},{6,0},{1,3},{3,5},{5,7},{7,1},{8,10},{10,12},{12... | collective-permute-start | bytes 294920 | tf_op jit(solution)/shard_map/ppermute | solution.py:185
  60.8 2.6 %collective-permute-start.2 = (f32[64,384]{1,0:T(8,128)S(1)}, f32[64,384]{1,0:T(8,128)S(1)}, u32[]{:S(2)}, u32[]{:S(2)}) collective-permute-start(f32[64,384]{1,0:T(8,128)S(1)} %get-tuple-element.32), channel_id=1, source_target_pairs={{0,4},{2,6},{4,0},{6,2},{1,5},{3,7},{5,1},{7,3},{8,12},{10,14},{12... | collective-permute-start | bytes 294920 | tf_op jit(solution)/shard_map/ppermute | solution.py:185
  63.4 1.1 collective-permute-start.3
  64.9 3.2 %collective-permute-done.2.refs_2_ = f32[64,384]{1,0:T(8,128)S(1)} collective-permute-done((f32[64,384]{1,0:T(8,128)S(1)}, f32[64,384]{1,0:T(8,128)S(1)}, u32[]{:S(2)}, u32[]{:S(2)}) %collective-permute-start.2) | collective-permute-done | bytes 98336 | tf_op jit(solution)/shard_map/ppermute | solution.py:185
  68.1 1.4 %shard_map.62 = (f32[64,384]{1,0:T(8,128)S(1)}, bf16[16,64,384]{2,1,0:T(8,128)(2,1)}, f32[1,128]{1,0:T(1,128)S(1)}) custom-call(f32[64,384]{1,0:T(8,128)S(1)} %get-tuple-element.30.refs_0_, f32[64,384]{1,0:T(8,128)S(1)} %collective-permute-done.1.refs_1_, f32[64,384]{1,0:T(8,128)S(1)} %collective-permute-done.2.refs_2_, ...), custom_call_target="tpu_custom_call" | custom-call | tf_op jit(solution)/shard_map/pallas_call | solution.py:352
  69.6 3.6 %all-to-all-start.1 = ((bf16[16,64,384]{2,1,0:T(8,128)(2,1)}), bf16[16,64,384]{2,1,0:T(8,128)(2,1)S(1)}, u32[]{:S(2)}, u32[]{:S(2)}) async-start(bf16[16,64,384]{2,1,0:T(8,128)(2,1)} %get-tuple-element.34), calls=%async_computation.1 | async-start | bytes 1572864 | tf_op jit(solution)/shard_map/all_to_all | solution.py:363
  73.2 14.5 %all-gather.1 = f32[512,384]{1,0:T(8,128)S(1)} all-gather(f32[64,384]{1,0:T(8,128)S(1)} %get-tuple-element.35.refs_5_), channel_id=3, replica_groups=mesh['row'=16,'y'=4,'core'=2] {'y','core'}, dimensions={0}, use_global_device_ids=true | all-gather | bytes 884736 | tf_op jit(solution)/shard_map/all_gather | solution.py:364
  87.7 10.5 %shard_map.63 = (f32[4,72,384]{2,1,0:T(8,128)S(1)}, f32[4,72,384]{2,1,0:T(8,128)S(1)}) custom-call(bf16[6144,3072]{1,0:T(8,128)(2,1)} %get-tuple-element.25.tile_ref, bf16[144,3072]{1,0:T(8,128)(2,1)S(1)} %get-tuple-element.26.right_ref, bf16[144,1536]{1,0:T(8,128)(2,1)S(1)} %get-tuple-element.27.left_ref, bf16[16,64,384]{2,1,0:T(8,128)(2,1)S(1)} %all-to-all-done.1.col_ref, ...), custom_call_target="tpu_custom_call" | custom-call | tf_op jit(solution)/shard_map/pallas_call | solution.py:368
  98.2 0.9 collective-permute-start.4
  99.1 1.4 %collective-permute-done.4.other_ref = f32[4,72,384]{2,1,0:T(8,128)S(1)} collective-permute-done((f32[4,72,384]{2,1,0:T(8,128)S(1)}, f32[4,72,384]{2,1,0:T(8,128)S(1)}, u32[]{:S(2)}, u32[]{:S(2)}) %collective-permute-start.4) | collective-permute-done | bytes 442400 | tf_op jit(solution)/shard_map/ppermute | solution.py:172
  101.2 9.0 %all-to-all-start.2 = ((f32[64,8,128]{2,1,0:T(8,128)}), f32[64,8,128]{2,1,0:T(8,128)S(1)}, u32[]{:S(2)}, u32[]{:S(2)}) async-start(f32[64,8,128]{2,1,0:T(8,128)} %get-tuple-element.43), calls=%async_computation.2 | async-start | bytes 524288 | tf_op jit(solution)/shard_map/all_to_all | solution.py:385
  110.2 1.1 collective-permute-start.5
  111.3 2.4 %collective-permute-start.6 = (f32[64,384]{1,0:T(8,128)S(1)}, f32[64,384]{1,0:T(8,128)S(1)}, u32[]{:S(2)}, u32[]{:S(2)}) collective-permute-start(f32[64,384]{1,0:T(8,128)S(1)} %get-tuple-element.41), channel_id=1, source_target_pairs={{0,4},{2,6},{4,0},{6,2},{1,5},{3,7},{5,1},{7,3},{8,12},{10,14},{12... | collective-permute-start | bytes 294920 | tf_op jit(solution)/shard_map/ppermute | solution.py:185
  113.7 1.2 collective-permute-start.7
  114.9 3.2 %collective-permute-done.5.refs_1_ = f32[64,384]{1,0:T(8,128)S(1)} collective-permute-done((f32[64,384]{1,0:T(8,128)S(1)}, f32[64,384]{1,0:T(8,128)S(1)}, u32[]{:S(2)}, u32[]{:S(2)}) %collective-permute-start.5) | collective-permute-done | bytes 98336 | tf_op jit(solution)/shard_map/ppermute | solution.py:185
  118.1 2.8 %collective-permute-done.6.refs_2_ = f32[64,384]{1,0:T(8,128)S(1)} collective-permute-done((f32[64,384]{1,0:T(8,128)S(1)}, f32[64,384]{1,0:T(8,128)S(1)}, u32[]{:S(2)}, u32[]{:S(2)}) %collective-permute-start.6) | collective-permute-done | bytes 98336 | tf_op jit(solution)/shard_map/ppermute | solution.py:185
  120.9 1.1 shard_map.65
  (13 shorter events, 1.2 us)
Async XLA Ops:
  3.2 8.6 %copy-start.2 = (bf16[64,384]{1,0:T(8,128)(2,1)S(1)}, bf16[64,384]{1,0:T(8,128)(2,1)}, u32[]{:S(2)}) copy-start(bf16[64,384]{1,0:T(8,128)(2,1)} %get-tuple-element.23) | copy-start | bytes 147460
  3.2 31.5 %all-to-all-start = ((bf16[16,128,384]{2,1,0:T(8,128)(2,1)}), bf16[16,128,384]{2,1,0:T(8,128)(2,1)S(1)}, u32[]{:S(2)}, u32[]{:S(2)}) async-start(bf16[16,128,384]{2,1,0:T(8,128)(2,1)} %get-tuple-element.24), calls=%async_computation | async-start | bytes 3145728 | tf_op jit(solution)/shard_map/all_to_all | solution.py:325
  11.8 56.3 %copy-start = (f32[64,384]{1,0:T(8,128)S(1)}, f32[64,384]{1,0:T(8,128)}, u32[]{:S(2)}) copy-start(f32[64,384]{1,0:T(8,128)} %refs_6_.1) | copy-start | bytes 294916
  11.8 56.3 %copy-start.1 = (s32[64,384]{1,0:T(8,128)S(1)}, s32[64,384]{1,0:T(8,128)}, u32[]{:S(2)}) copy-start(s32[64,384]{1,0:T(8,128)} %refs_7_.1) | copy-start | bytes 294916
  55.5 3.9 %collective-permute-start = (f32[4,64,384]{2,1,0:T(8,128)S(1)}, f32[4,64,384]{2,1,0:T(8,128)S(1)}, u32[]{:S(2)}, u32[]{:S(2)}) collective-permute-start(f32[4,64,384]{2,1,0:T(8,128)S(1)} %get-tuple-element.29), channel_id=1, source_target_pairs={{0,1},{1,0},{2,3},{3,2},{4,5},{5,4},{6,7},{7,6},{8,9},{9,8},{10,11... | collective-permute-start | bytes 1179656 | tf_op jit(solution)/shard_map/ppermute | solution.py:172
  59.4 5.4 %collective-permute-start.1 = (f32[64,384]{1,0:T(8,128)S(1)}, f32[64,384]{1,0:T(8,128)S(1)}, u32[]{:S(2)}, u32[]{:S(2)}) collective-permute-start(f32[64,384]{1,0:T(8,128)S(1)} %get-tuple-element.31), channel_id=1, source_target_pairs={{0,2},{2,4},{4,6},{6,0},{1,3},{3,5},{5,7},{7,1},{8,10},{10,12},{12... | collective-permute-start | bytes 294920 | tf_op jit(solution)/shard_map/ppermute | solution.py:185
  60.8 7.3 %collective-permute-start.2 = (f32[64,384]{1,0:T(8,128)S(1)}, f32[64,384]{1,0:T(8,128)S(1)}, u32[]{:S(2)}, u32[]{:S(2)}) collective-permute-start(f32[64,384]{1,0:T(8,128)S(1)} %get-tuple-element.32), channel_id=1, source_target_pairs={{0,4},{2,6},{4,0},{6,2},{1,5},{3,7},{5,1},{7,3},{8,12},{10,14},{12... | collective-permute-start | bytes 294920 | tf_op jit(solution)/shard_map/ppermute | solution.py:185
  63.4 4.7 %collective-permute-start.3 = (f32[64,384]{1,0:T(8,128)S(1)}, f32[64,384]{1,0:T(8,128)S(1)}, u32[]{:S(2)}, u32[]{:S(2)}) collective-permute-start(f32[64,384]{1,0:T(8,128)S(1)} %get-tuple-element.33), channel_id=1, source_target_pairs={{0,6},{2,0},{4,2},{6,4},{1,7},{3,1},{5,3},{7,5},{8,14},{10,8},{12,... | collective-permute-start | bytes 294920 | tf_op jit(solution)/shard_map/ppermute | solution.py:185
  69.6 18.2 %all-to-all-start.1 = ((bf16[16,64,384]{2,1,0:T(8,128)(2,1)}), bf16[16,64,384]{2,1,0:T(8,128)(2,1)S(1)}, u32[]{:S(2)}, u32[]{:S(2)}) async-start(bf16[16,64,384]{2,1,0:T(8,128)(2,1)} %get-tuple-element.34), calls=%async_computation.1 | async-start | bytes 1572864 | tf_op jit(solution)/shard_map/all_to_all | solution.py:363
  98.2 2.3 %collective-permute-start.4 = (f32[4,72,384]{2,1,0:T(8,128)S(1)}, f32[4,72,384]{2,1,0:T(8,128)S(1)}, u32[]{:S(2)}, u32[]{:S(2)}) collective-permute-start(f32[4,72,384]{2,1,0:T(8,128)S(1)} %get-tuple-element.38), channel_id=1, source_target_pairs={{0,1},{1,0},{2,3},{3,2},{4,5},{5,4},{6,7},{7,6},{8,9},{9,8},{10,11... | collective-permute-start | bytes 1327112 | tf_op jit(solution)/shard_map/ppermute | solution.py:172
  101.2 19.7 %all-to-all-start.2 = ((f32[64,8,128]{2,1,0:T(8,128)}), f32[64,8,128]{2,1,0:T(8,128)S(1)}, u32[]{:S(2)}, u32[]{:S(2)}) async-start(f32[64,8,128]{2,1,0:T(8,128)} %get-tuple-element.43), calls=%async_computation.2 | async-start | bytes 524288 | tf_op jit(solution)/shard_map/all_to_all | solution.py:385
  110.2 7.8 %collective-permute-start.5 = (f32[64,384]{1,0:T(8,128)S(1)}, f32[64,384]{1,0:T(8,128)S(1)}, u32[]{:S(2)}, u32[]{:S(2)}) collective-permute-start(f32[64,384]{1,0:T(8,128)S(1)} %get-tuple-element.40), channel_id=1, source_target_pairs={{0,2},{2,4},{4,6},{6,0},{1,3},{3,5},{5,7},{7,1},{8,10},{10,12},{12... | collective-permute-start | bytes 294920 | tf_op jit(solution)/shard_map/ppermute | solution.py:185
  111.3 9.5 %collective-permute-start.6 = (f32[64,384]{1,0:T(8,128)S(1)}, f32[64,384]{1,0:T(8,128)S(1)}, u32[]{:S(2)}, u32[]{:S(2)}) collective-permute-start(f32[64,384]{1,0:T(8,128)S(1)} %get-tuple-element.41), channel_id=1, source_target_pairs={{0,4},{2,6},{4,0},{6,2},{1,5},{3,7},{5,1},{7,3},{8,12},{10,14},{12... | collective-permute-start | bytes 294920 | tf_op jit(solution)/shard_map/ppermute | solution.py:185
  113.7 7.2 %collective-permute-start.7 = (f32[64,384]{1,0:T(8,128)S(1)}, f32[64,384]{1,0:T(8,128)S(1)}, u32[]{:S(2)}, u32[]{:S(2)}) collective-permute-start(f32[64,384]{1,0:T(8,128)S(1)} %get-tuple-element.42), channel_id=1, source_target_pairs={{0,6},{2,0},{4,2},{6,4},{1,7},{3,1},{5,3},{7,5},{8,14},{10,8},{12,... | collective-permute-start | bytes 294920 | tf_op jit(solution)/shard_map/ppermute | solution.py:185
where the time goes:
time: 122 us
  Pallas kernels  37.2 us (30%)
  starting transfers between devices  34.3 us (28%)
  blocking collectives  28.9 us (24%)
  waiting for transfers between devices  20.8 us (17%)
    pallas_call x1, Pallas kernels, shards(): pl.pallas_call(functools.partial(block_kernel, step_rows), grid=(rows * w...  20.9 us
    all_gather x1, blocking collectives, shards(): row_images = lax.all_gather(image, COL)  14.5 us
    all_gather x1, blocking collectives, shards(): row_feats = lax.all_gather(feats, COL)  14.4 us
    pallas_call x1, Pallas kernels, shards(): pl.pallas_call(functools.partial(again_kernel, again_rows), out_shape=(ha...  10.5 us
    ppermute x6, starting transfers between devices, exchange(): lax.ppermute(term, 'y', [(k, (k + shift) % count) for k in range(count)])  9.72 us
    ppermute x6, waiting for transfers between devices, exchange(): lax.ppermute(term, 'y', [(k, (k + shift) % count) for k in range(count)])  9.55 us
    all_to_all x1, starting transfers between devices, shards(): sums = lax.all_to_all(sums, ('row', 'y'), 0, 0)  9.02 us
    all_to_all x1, starting transfers between devices, shards(): col_pack = lax.all_to_all(pack, 'row', 0, 0)  8.57 us
  transfers between devices with their start and end apart: 11, of which 7 were waited for; matrix products, arithmetic and copies ran while one was open for 0% of the time, Pallas kernels for 0%

commit v1 on v0

--- a/solution.py
+++ b/solution.py
@@ -10,7 +10,7 @@
 
 noise_level = 0.5
 AGAIN = 2
-FAT = 8
+SUM_ROWS = 4
 COL = ("y", "core")
 VMEM = pl.BlockSpec(memory_space=pltpu.VMEM)
 bf16 = jnp.bfloat16
@@ -164,7 +164,7 @@
         out_ref[...] = mine_ref[place, 0:epochs, :] + other_ref[place, 0:epochs, :]
     for sums_ref in out_refs[count:]:
         row = mine_ref[0, epochs:, 0:128] + other_ref[0, epochs:, 0:128]
-        sums_ref[...] = jnp.broadcast_to(row[None], sums_ref.shape)
+        sums_ref[...] = jnp.broadcast_to(row[None, 0:SUM_ROWS], sums_ref.shape)
 
 
 def pair_sum(mine, other, block, *more):
@@ -380,7 +380,7 @@
     )(tile, right, left, col_weighted, row_images, sums)
 
     *terms, sums = pair_sum(
-        mine, other, field, jax.ShapeDtypeStruct((rows * ys, FAT, 128), f32)
+        mine, other, field, jax.ShapeDtypeStruct((rows * ys, SUM_ROWS, 128), f32)
     )
     sums = lax.all_to_all(sums, ("row", "y"), 0, 0)
     terms = exchange(terms)

time: 122 us -> 121 us (level)
  waiting for transfers between devices: 20.8 us -> 19.3 us
    ppermute x6, waiting for transfers between devices: 9.55 us -> 8.05 us  [exchange(): lax.ppermute(term, 'y', [(k, (k + shift) % count) for k in range(count)])]
where the time goes in v1:
time: 121 us; the launch traced here: 120 us
  Pallas kernels  37.1 us (31%)
  starting transfers between devices  34.3 us (28%)
  blocking collectives  28.9 us (24%)
  waiting for transfers between devices  19.3 us (16%)
    pallas_call x1, Pallas kernels, shards(): pl.pallas_call(functools.partial(block_kernel, step_rows), grid=(rows * w...  20.9 us
    all_gather x1, blocking collectives, shards(): row_images = lax.all_gather(image, COL)  14.5 us
    all_gather x1, blocking collectives, shards(): row_feats = lax.all_gather(feats, COL)  14.4 us
    pallas_call x1, Pallas kernels, shards(): pl.pallas_call(functools.partial(again_kernel, again_rows), out_shape=(ha...  10.5 us
    ppermute x6, starting transfers between devices, exchange(): lax.ppermute(term, 'y', [(k, (k + shift) % count) for k in range(count)])  9.72 us
    all_to_all x1, starting transfers between devices, shards(): sums = lax.all_to_all(sums, ('row', 'y'), 0, 0)  9.02 us
    all_to_all x1, starting transfers between devices, shards(): col_pack = lax.all_to_all(pack, 'row', 0, 0)  8.57 us
    all_to_all x1, waiting for transfers between devices, shards(): col_pack = lax.all_to_all(pack, 'row', 0, 0)  8.45 us
  transfers between devices with their start and end apart: 11, of which 7 were waited for; matrix products, arithmetic and copies ran while one was open for 0% of the time, Pallas kernels for 0%

profile of v1, /device:TPU:1, one launch (start us, length us, event | category | flops | bytes accessed | tf_op | source)
XLA Modules:
  0.0 120.4 jit_solution(383361327149277451)
XLA Ops:
  0.6 2.5 %shard_map.59 = (bf16[64,384]{1,0:T(8,128)(2,1)}, bf16[16,128,384]{2,1,0:T(8,128)(2,1)}) custom-call(f32[32,384]{1,0:T(8,128)} %feat_in.1, f32[1,32]{1,0:T(1,128)} %bitcast.5, f32[64,384]{1,0:T(8,128)} %refs_6_.1, s32[64,384]{1,0:T(8,128)} %refs_7_.1), custom_call_target="tpu_custom_call" | custom-call | tf_op jit(solution)/shard_map/pallas_call | solution.py:304
  3.2 8.6 %all-to-all-start = ((bf16[16,128,384]{2,1,0:T(8,128)(2,1)}), bf16[16,128,384]{2,1,0:T(8,128)(2,1)S(1)}, u32[]{:S(2)}, u32[]{:S(2)}) async-start(bf16[16,128,384]{2,1,0:T(8,128)(2,1)} %get-tuple-element.24), calls=%async_computation | async-start | bytes 3145728 | tf_op jit(solution)/shard_map/all_to_all | solution.py:325
  11.8 14.4 %all-gather = bf16[512,384]{1,0:T(8,128)(2,1)S(1)} all-gather(bf16[64,384]{1,0:T(8,128)(2,1)S(1)} %copy-done.2), channel_id=2, replica_groups=mesh['row'=16,'y'=4,'core'=2] {'y','core'}, dimensions={0}, use_global_device_ids=true | all-gather | bytes 442368 | tf_op jit(solution)/shard_map/all_gather | solution.py:326
  26.2 8.4 %all-to-all-done.col_ref = bf16[16,128,384]{2,1,0:T(8,128)(2,1)S(1)} async-done(((bf16[16,128,384]{2,1,0:T(8,128)(2,1)}), bf16[16,128,384]{2,1,0:T(8,128)(2,1)S(1)}, u32[]{:S(2)}, u32[]{:S(2)}) %all-to-all-start) | async-done | bytes 1572896 | tf_op jit(solution)/shard_map/all_to_all | solution.py:325
  34.7 20.9 %shard_map.60 = (bf16[6144,3072]{1,0:T(8,128)(2,1)}, bf16[144,3072]{1,0:T(8,128)(2,1)S(1)}, bf16[144,1536]{1,0:T(8,128)(2,1)S(1)}, f32[4,64,384]{2,1,0:T(8,128)S(1)}, f32[4,64,384]{2,1,0:T(8,128)S(1)}) custom-call(bf16[8,64,384]{2,1,0:T(8,128)(2,1)S(1)} %bitcast.4, bf16[16,128,384]{2,1,0:T(8,128)(2,1)S(1)} %all-to-all-done.col_ref), custom_call_target="tpu_custom_call" | custom-call | tf_op jit(solution)/shard_map/pallas_call | solution.py:331
  55.5 2.5 %collective-permute-start = (f32[4,64,384]{2,1,0:T(8,128)S(1)}, f32[4,64,384]{2,1,0:T(8,128)S(1)}, u32[]{:S(2)}, u32[]{:S(2)}) collective-permute-start(f32[4,64,384]{2,1,0:T(8,128)S(1)} %get-tuple-element.29), channel_id=1, source_target_pairs={{0,1},{1,0},{2,3},{3,2},{4,5},{5,4},{6,7},{7,6},{8,9},{9,8},{10,11... | collective-permute-start | bytes 1179656 | tf_op jit(solution)/shard_map/ppermute | solution.py:172
  58.1 1.3 %collective-permute-done.other_ref = f32[4,64,384]{2,1,0:T(8,128)S(1)} collective-permute-done((f32[4,64,384]{2,1,0:T(8,128)S(1)}, f32[4,64,384]{2,1,0:T(8,128)S(1)}, u32[]{:S(2)}, u32[]{:S(2)}) %collective-permute-start) | collective-permute-done | bytes 393248 | tf_op jit(solution)/shard_map/ppermute | solution.py:172
  59.4 1.4 %collective-permute-start.1 = (f32[64,384]{1,0:T(8,128)S(1)}, f32[64,384]{1,0:T(8,128)S(1)}, u32[]{:S(2)}, u32[]{:S(2)}) collective-permute-start(f32[64,384]{1,0:T(8,128)S(1)} %get-tuple-element.31), channel_id=1, source_target_pairs={{0,2},{2,4},{4,6},{6,0},{1,3},{3,5},{5,7},{7,1},{8,10},{10,12},{12... | collective-permute-start | bytes 294920 | tf_op jit(solution)/shard_map/ppermute | solution.py:185
  60.8 2.6 %collective-permute-start.2 = (f32[64,384]{1,0:T(8,128)S(1)}, f32[64,384]{1,0:T(8,128)S(1)}, u32[]{:S(2)}, u32[]{:S(2)}) collective-permute-start(f32[64,384]{1,0:T(8,128)S(1)} %get-tuple-element.32), channel_id=1, source_target_pairs={{0,4},{2,6},{4,0},{6,2},{1,5},{3,7},{5,1},{7,3},{8,12},{10,14},{12... | collective-permute-start | bytes 294920 | tf_op jit(solution)/shard_map/ppermute | solution.py:185
  63.4 1.1 collective-permute-start.3
  64.9 3.2 %collective-permute-done.2.refs_2_ = f32[64,384]{1,0:T(8,128)S(1)} collective-permute-done((f32[64,384]{1,0:T(8,128)S(1)}, f32[64,384]{1,0:T(8,128)S(1)}, u32[]{:S(2)}, u32[]{:S(2)}) %collective-permute-start.2) | collective-permute-done | bytes 98336 | tf_op jit(solution)/shard_map/ppermute | solution.py:185
  68.1 1.4 %shard_map.62 = (f32[64,384]{1,0:T(8,128)S(1)}, bf16[16,64,384]{2,1,0:T(8,128)(2,1)}, f32[1,128]{1,0:T(1,128)S(1)}) custom-call(f32[64,384]{1,0:T(8,128)S(1)} %get-tuple-element.30.refs_0_, f32[64,384]{1,0:T(8,128)S(1)} %collective-permute-done.1.refs_1_, f32[64,384]{1,0:T(8,128)S(1)} %collective-permute-done.2.refs_2_, ...), custom_call_target="tpu_custom_call" | custom-call | tf_op jit(solution)/shard_map/pallas_call | solution.py:352
  69.6 3.6 %all-to-all-start.1 = ((bf16[16,64,384]{2,1,0:T(8,128)(2,1)}), bf16[16,64,384]{2,1,0:T(8,128)(2,1)S(1)}, u32[]{:S(2)}, u32[]{:S(2)}) async-start(bf16[16,64,384]{2,1,0:T(8,128)(2,1)} %get-tuple-element.34), calls=%async_computation.1 | async-start | bytes 1572864 | tf_op jit(solution)/shard_map/all_to_all | solution.py:363
  73.2 14.5 %all-gather.1 = f32[512,384]{1,0:T(8,128)S(1)} all-gather(f32[64,384]{1,0:T(8,128)S(1)} %get-tuple-element.35.refs_5_), channel_id=3, replica_groups=mesh['row'=16,'y'=4,'core'=2] {'y','core'}, dimensions={0}, use_global_device_ids=true | all-gather | bytes 884736 | tf_op jit(solution)/shard_map/all_gather | solution.py:364
  87.7 10.5 %shard_map.63 = (f32[4,72,384]{2,1,0:T(8,128)S(1)}, f32[4,72,384]{2,1,0:T(8,128)S(1)}) custom-call(bf16[6144,3072]{1,0:T(8,128)(2,1)} %get-tuple-element.25.tile_ref, bf16[144,3072]{1,0:T(8,128)(2,1)S(1)} %get-tuple-element.26.right_ref, bf16[144,1536]{1,0:T(8,128)(2,1)S(1)} %get-tuple-element.27.left_ref, bf16[16,64,384]{2,1,0:T(8,128)(2,1)S(1)} %all-to-all-done.1.col_ref, ...), custom_call_target="tpu_custom_call" | custom-call | tf_op jit(solution)/shard_map/pallas_call | solution.py:368
  98.2 0.9 collective-permute-start.4
  99.1 1.4 %collective-permute-done.4.other_ref = f32[4,72,384]{2,1,0:T(8,128)S(1)} collective-permute-done((f32[4,72,384]{2,1,0:T(8,128)S(1)}, f32[4,72,384]{2,1,0:T(8,128)S(1)}, u32[]{:S(2)}, u32[]{:S(2)}) %collective-permute-start.4) | collective-permute-done | bytes 442400 | tf_op jit(solution)/shard_map/ppermute | solution.py:172
  101.2 9.0 %all-to-all-start.2 = ((f32[64,4,128]{2,1,0:T(4,128)}), f32[64,4,128]{2,1,0:T(4,128)S(1)}, u32[]{:S(2)}, u32[]{:S(2)}) async-start(f32[64,4,128]{2,1,0:T(4,128)} %get-tuple-element.43), calls=%async_computation.2 | async-start | bytes 262144 | tf_op jit(solution)/shard_map/all_to_all | solution.py:385
  110.2 1.1 collective-permute-start.5
  111.3 2.4 %collective-permute-start.6 = (f32[64,384]{1,0:T(8,128)S(1)}, f32[64,384]{1,0:T(8,128)S(1)}, u32[]{:S(2)}, u32[]{:S(2)}) collective-permute-start(f32[64,384]{1,0:T(8,128)S(1)} %get-tuple-element.41), channel_id=1, source_target_pairs={{0,4},{2,6},{4,0},{6,2},{1,5},{3,7},{5,1},{7,3},{8,12},{10,14},{12... | collective-permute-start | bytes 294920 | tf_op jit(solution)/shard_map/ppermute | solution.py:185
  113.7 1.2 collective-permute-start.7
  114.8 1.6 %collective-permute-done.5.refs_1_ = f32[64,384]{1,0:T(8,128)S(1)} collective-permute-done((f32[64,384]{1,0:T(8,128)S(1)}, f32[64,384]{1,0:T(8,128)S(1)}, u32[]{:S(2)}, u32[]{:S(2)}) %collective-permute-start.5) | collective-permute-done | bytes 98336 | tf_op jit(solution)/shard_map/ppermute | solution.py:185
  116.5 2.8 %collective-permute-done.6.refs_2_ = f32[64,384]{1,0:T(8,128)S(1)} collective-permute-done((f32[64,384]{1,0:T(8,128)S(1)}, f32[64,384]{1,0:T(8,128)S(1)}, u32[]{:S(2)}, u32[]{:S(2)}) %collective-permute-start.6) | collective-permute-done | bytes 98336 | tf_op jit(solution)/shard_map/ppermute | solution.py:185
  119.3 1.1 shard_map.65
  (13 shorter events, 1.1 us)
Async XLA Ops:
  3.2 8.6 %copy-start.2 = (bf16[64,384]{1,0:T(8,128)(2,1)S(1)}, bf16[64,384]{1,0:T(8,128)(2,1)}, u32[]{:S(2)}) copy-start(bf16[64,384]{1,0:T(8,128)(2,1)} %get-tuple-element.23) | copy-start | bytes 147460
  3.2 31.5 %all-to-all-start = ((bf16[16,128,384]{2,1,0:T(8,128)(2,1)}), bf16[16,128,384]{2,1,0:T(8,128)(2,1)S(1)}, u32[]{:S(2)}, u32[]{:S(2)}) async-start(bf16[16,128,384]{2,1,0:T(8,128)(2,1)} %get-tuple-element.24), calls=%async_computation | async-start | bytes 3145728 | tf_op jit(solution)/shard_map/all_to_all | solution.py:325
  11.8 56.3 %copy-start = (f32[64,384]{1,0:T(8,128)S(1)}, f32[64,384]{1,0:T(8,128)}, u32[]{:S(2)}) copy-start(f32[64,384]{1,0:T(8,128)} %refs_6_.1) | copy-start | bytes 294916
  11.8 56.3 %copy-start.1 = (s32[64,384]{1,0:T(8,128)S(1)}, s32[64,384]{1,0:T(8,128)}, u32[]{:S(2)}) copy-start(s32[64,384]{1,0:T(8,128)} %refs_7_.1) | copy-start | bytes 294916
  55.5 3.9 %collective-permute-start = (f32[4,64,384]{2,1,0:T(8,128)S(1)}, f32[4,64,384]{2,1,0:T(8,128)S(1)}, u32[]{:S(2)}, u32[]{:S(2)}) collective-permute-start(f32[4,64,384]{2,1,0:T(8,128)S(1)} %get-tuple-element.29), channel_id=1, source_target_pairs={{0,1},{1,0},{2,3},{3,2},{4,5},{5,4},{6,7},{7,6},{8,9},{9,8},{10,11... | collective-permute-start | bytes 1179656 | tf_op jit(solution)/shard_map/ppermute | solution.py:172
  59.4 5.4 %collective-permute-start.1 = (f32[64,384]{1,0:T(8,128)S(1)}, f32[64,384]{1,0:T(8,128)S(1)}, u32[]{:S(2)}, u32[]{:S(2)}) collective-permute-start(f32[64,384]{1,0:T(8,128)S(1)} %get-tuple-element.31), channel_id=1, source_target_pairs={{0,2},{2,4},{4,6},{6,0},{1,3},{3,5},{5,7},{7,1},{8,10},{10,12},{12... | collective-permute-start | bytes 294920 | tf_op jit(solution)/shard_map/ppermute | solution.py:185
  60.8 7.3 %collective-permute-start.2 = (f32[64,384]{1,0:T(8,128)S(1)}, f32[64,384]{1,0:T(8,128)S(1)}, u32[]{:S(2)}, u32[]{:S(2)}) collective-permute-start(f32[64,384]{1,0:T(8,128)S(1)} %get-tuple-element.32), channel_id=1, source_target_pairs={{0,4},{2,6},{4,0},{6,2},{1,5},{3,7},{5,1},{7,3},{8,12},{10,14},{12... | collective-permute-start | bytes 294920 | tf_op jit(solution)/shard_map/ppermute | solution.py:185
  63.4 4.7 %collective-permute-start.3 = (f32[64,384]{1,0:T(8,128)S(1)}, f32[64,384]{1,0:T(8,128)S(1)}, u32[]{:S(2)}, u32[]{:S(2)}) collective-permute-start(f32[64,384]{1,0:T(8,128)S(1)} %get-tuple-element.33), channel_id=1, source_target_pairs={{0,6},{2,0},{4,2},{6,4},{1,7},{3,1},{5,3},{7,5},{8,14},{10,8},{12,... | collective-permute-start | bytes 294920 | tf_op jit(solution)/shard_map/ppermute | solution.py:185
  69.6 18.2 %all-to-all-start.1 = ((bf16[16,64,384]{2,1,0:T(8,128)(2,1)}), bf16[16,64,384]{2,1,0:T(8,128)(2,1)S(1)}, u32[]{:S(2)}, u32[]{:S(2)}) async-start(bf16[16,64,384]{2,1,0:T(8,128)(2,1)} %get-tuple-element.34), calls=%async_computation.1 | async-start | bytes 1572864 | tf_op jit(solution)/shard_map/all_to_all | solution.py:363
  98.2 2.3 %collective-permute-start.4 = (f32[4,72,384]{2,1,0:T(8,128)S(1)}, f32[4,72,384]{2,1,0:T(8,128)S(1)}, u32[]{:S(2)}, u32[]{:S(2)}) collective-permute-start(f32[4,72,384]{2,1,0:T(8,128)S(1)} %get-tuple-element.38), channel_id=1, source_target_pairs={{0,1},{1,0},{2,3},{3,2},{4,5},{5,4},{6,7},{7,6},{8,9},{9,8},{10,11... | collective-permute-start | bytes 1327112 | tf_op jit(solution)/shard_map/ppermute | solution.py:172
  101.2 18.2 %all-to-all-start.2 = ((f32[64,4,128]{2,1,0:T(4,128)}), f32[64,4,128]{2,1,0:T(4,128)S(1)}, u32[]{:S(2)}, u32[]{:S(2)}) async-start(f32[64,4,128]{2,1,0:T(4,128)} %get-tuple-element.43), calls=%async_computation.2 | async-start | bytes 262144 | tf_op jit(solution)/shard_map/all_to_all | solution.py:385
  110.2 6.3 %collective-permute-start.5 = (f32[64,384]{1,0:T(8,128)S(1)}, f32[64,384]{1,0:T(8,128)S(1)}, u32[]{:S(2)}, u32[]{:S(2)}) collective-permute-start(f32[64,384]{1,0:T(8,128)S(1)} %get-tuple-element.40), channel_id=1, source_target_pairs={{0,2},{2,4},{4,6},{6,0},{1,3},{3,5},{5,7},{7,1},{8,10},{10,12},{12... | collective-permute-start | bytes 294920 | tf_op jit(solution)/shard_map/ppermute | solution.py:185
  111.3 8.0 %collective-permute-start.6 = (f32[64,384]{1,0:T(8,128)S(1)}, f32[64,384]{1,0:T(8,128)S(1)}, u32[]{:S(2)}, u32[]{:S(2)}) collective-permute-start(f32[64,384]{1,0:T(8,128)S(1)} %get-tuple-element.41), channel_id=1, source_target_pairs={{0,4},{2,6},{4,0},{6,2},{1,5},{3,7},{5,1},{7,3},{8,12},{10,14},{12... | collective-permute-start | bytes 294920 | tf_op jit(solution)/shard_map/ppermute | solution.py:185
  113.7 5.7 %collective-permute-start.7 = (f32[64,384]{1,0:T(8,128)S(1)}, f32[64,384]{1,0:T(8,128)S(1)}, u32[]{:S(2)}, u32[]{:S(2)}) collective-permute-start(f32[64,384]{1,0:T(8,128)S(1)} %get-tuple-element.42), channel_id=1, source_target_pairs={{0,6},{2,0},{4,2},{6,4},{1,7},{3,1},{5,3},{7,5},{8,14},{10,8},{12,... | collective-permute-start | bytes 294920 | tf_op jit(solution)/shard_map/ppermute | solution.py:185
